TPU v7x, 32 devices: a whole 2x2x4 slice. The times are simulated.
32 devices in a mesh: blk: 8 (over z, core), rep: 4 (over y, x).
Axes of the slice: x: 2, y: 2, z: 4, core: 2. Of those that a mesh axis runs over, the one named last changes fastest.
Arguments:
- features: bfloat16 [32768, 256], P('blk'), may hold values from -6 to 6
- state: bfloat16 [32768, 256], P('blk'), may hold values from -1 to 1
- tiles: bfloat16 [8, 8, 64, 128, 128], P('blk', 'rep'), may hold values from -0.25 to 0.25
- tile_count: int32 [8, 8], P('blk', 'rep'), may hold values from 0 to 64, as said below
- tile_rows: int32 [8, 8, 64], P('blk', 'rep'), may hold values from 0 to 31, as said below
- tile_cols: int32 [8, 8, 64], P('blk', 'rep'), may hold values from 0 to 31, as said below
- w_graph: bfloat16 [256, 256], replicated, may hold values from -0.375 to 0.375
- b_graph: float32 [256], replicated, may hold values from -1 to 1
- w_input: bfloat16 [256, 768], replicated, may hold values from -0.375 to 0.375
- w_state: bfloat16 [256, 512], replicated, may hold values from -0.375 to 0.375
- w_cand: bfloat16 [256, 256], replicated, may hold values from -0.375 to 0.375
- b_gates: float32 [768], replicated, may hold values from -1 to 1
- cotangent: bfloat16 [32768, 256], P('blk'), may hold values from -6 to 6
Outputs:
- new_state: bfloat16 [32768, 256], P('blk')
- state_grad: bfloat16 [32768, 256], P('blk')
- grad_graph: float32 [256, 256], replicated
- grad_graph_bias: float32 [256], replicated
- grad_input: float32 [256, 768], replicated
- grad_state: float32 [256, 512], replicated
- grad_cand: float32 [256, 256], replicated
- grad_gates: float32 [768], replicated
Inputs may be any that keep to these rules, and one draw needn't show every extreme that they name: Only the first tile_count[b, s] entries of a section list are used; some list holds exactly 64 tiles in every draw, and some lists are empty. `tile_rows`: row tile of a list entry; the (row, column) positions within one list are distinct. `tile_cols`: column tile of a list entry within its section's block of nodes.
All inputs are finite; a program needn't handle non-finite values.
Results may differ from a plain program's by a relative error of at most 0.02.
Values may be sent and summed in bfloat16 or wider, within the bound.
A program may use at most 128 MiB of HBM per device.

v0:
```python
import functools

import jax
import jax.numpy as jnp
from jax import lax
from jax.experimental import pallas as pl
from jax.experimental.pallas import tpu as pltpu
from jax.sharding import PartitionSpec as P

MESH = pl.DeviceIdType.MESH
CHUNKS = 16
AHEAD = 3
GROUP = 8
ROW_BLOCK = 256
VMEM_LIMIT = 56 * 1024 * 1024


def contract_first(left, right):
    return lax.dot_general(
        left, right, (((0,), (0,)), ((), ())), preferred_element_type=jnp.float32
    )


def contract_last(left, right):
    return lax.dot_general(
        left, right, (((1,), (1,)), ((), ())), preferred_element_type=jnp.float32
    )


def product(left, right):
    return jnp.dot(left, right, preferred_element_type=jnp.float32)


def rep_shift(rep, reps, k):
    return ((rep // 2 + k // 2) % (reps // 2)) * 2 + (rep % 2 + k % 2) % 2


def rep_origin(rep, reps, k):
    return ((rep // 2 + reps // 2 - k // 2) % (reps // 2)) * 2 + (rep % 2 + k % 2) % 2


def spread_kernel(chips, reps, lane, reduces, *refs):
    if reduces:
        feat, partial, early, out, s_all = refs[:5]
        sems = refs[5:]
        part_own, part_recv, part_sem, rs_send, rs_recv, ag_send, ag_recv = sems[6:]
    else:
        feat, out, early = refs[:3]
        sems = refs[3:]
        early_up, early_down, early_recv, early_own = sems[6:]
    up_sem, down_sem, recv_sem, pair_sem, pair_recv, own_sem = sems[:6]
    blk = lax.axis_index("blk")
    rep = lax.axis_index("rep")
    core = blk % 2
    chip = blk // 2
    above = (chip + 1) % chips
    below = (chip + chips - 1) % chips
    chunk = feat.shape[0] // CHUNKS
    lanes = out.shape[2]
    is_owner = chip == rep
    not_owner = chip != rep
    has_up = jnp.logical_and(chip >= rep, chip < chips - 1)
    has_down = jnp.logical_and(chip <= rep, chip > 0)
    away = jnp.maximum(chip - rep, rep - chip)

    def ahead(hop):
        return jnp.minimum(jnp.maximum(AHEAD * (chips - 2 - hop), 0), CHUNKS)

    sent = ahead(away)
    held = ahead(away - 1)

    def rows_of(j):
        return pl.ds(pl.multiple_of(j * chunk, chunk), chunk)

    def own(j):
        return pltpu.make_async_copy(
            feat.at[rows_of(j), pl.ds(lane, lanes)], out.at[core, rows_of(j)], own_sem.at[j]
        )

    def load(j, carry):
        own(j).start()
        return carry

    @pl.when(is_owner)
    def _():
        lax.fori_loop(0, CHUNKS, load, 0)

    if reduces:
        def held_copy(j):
            return pltpu.make_async_copy(
                early.at[rows_of(j)], out.at[core, rows_of(j)], own_sem.at[j]
            )

        def load_held(j, carry):
            held_copy(j).start()
            return carry

        @pl.when(not_owner)
        def _():
            lax.fori_loop(0, held, load_held, 0)

    else:
        def early_load(j):
            return pltpu.make_async_copy(
                feat.at[rows_of(j), pl.ds(lane + lanes, lanes)],
                early.at[rows_of(j)],
                early_own.at[j],
            )

        def load_early(j, carry):
            early_load(j).start()
            return carry

        @pl.when(is_owner)
        def _():
            lax.fori_loop(0, sent, load_early, 0)

    def remote(src, dst, send_sem, recv_sem, target):
        return pltpu.make_async_remote_copy(
            src_ref=src,
            dst_ref=dst,
            send_sem=send_sem,
            recv_sem=recv_sem,
            device_id=target,
            device_id_type=MESH,
        )

    def send(j, target, send_sem, got):
        here = out.at[core, rows_of(j)]
        return remote(here, here, send_sem.at[j], got.at[j], {"blk": target, "rep": rep})

    def up(j):
        return send(j, above * 2 + core, up_sem, recv_sem)

    def down(j):
        return send(j, below * 2 + core, down_sem, recv_sem)

    def pair(j):
        return send(j, chip * 2 + 1 - core, pair_sem, pair_recv)

    others = range(1, reps)
    targets = [
        {"blk": other, "rep": rep}
        for other in (above * 2 + core, below * 2 + core, chip * 2 + 1 - core)
    ]
    if reduces:
        targets += [{"blk": blk, "rep": rep_shift(rep, reps, k)} for k in others]
    barrier = pltpu.get_barrier_semaphore()
    for target in targets:
        pl.semaphore_signal(barrier, inc=1, device_id=target, device_id_type=MESH)
    pl.semaphore_wait(barrier, len(targets))

    if reduces:
        part_rows = partial.shape[0] // reps

        def part(index):
            return pl.ds(pl.multiple_of(index * part_rows, part_rows), part_rows)

        load_own = pltpu.make_async_copy(partial.at[part(rep)], part_own, part_sem)
        load_own.start()
        scatter = [
            remote(
                partial.at[part(rep_shift(rep, reps, k))],
                part_recv.at[k - 1],
                rs_send.at[k - 1],
                rs_recv.at[k - 1],
                {"blk": blk, "rep": rep_shift(rep, reps, k)},
            )
            for k in others
        ]
        gather = [
            remote(
                s_all.at[part(rep)],
                s_all.at[part(rep)],
                ag_send.at[k - 1],
                ag_recv.at[k - 1],
                {"blk": blk, "rep": rep_shift(rep, reps, k)},
            )
            for k in others
        ]
        for copy in reversed(scatter):
            copy.start()

    first = sent if reduces else 0
    ready = held if reduces else 0

    def step(j, carry):
        @pl.when(is_owner)
        def _():
            own(j).wait()

        if reduces:
            @pl.when(jnp.logical_and(not_owner, j < ready))
            def _():
                held_copy(j).wait()

        @pl.when(jnp.logical_and(not_owner, j >= ready))
        def _():
            up(j).wait_recv()

        @pl.when(jnp.logical_and(has_up, j >= first))
        def _():
            up(j).start()

        @pl.when(jnp.logical_and(has_down, j >= first))
        def _():
            down(j).start()

        pair(j).start()
        return carry

    if reduces:
        middle = jnp.where(is_owner, CHUNKS, jnp.minimum(CHUNKS, held + CHUNKS // 2))
    else:
        middle = CHUNKS
    lax.fori_loop(0, middle, step, 0)
    if not reduces:

        def early_to(j, target, send_sem):
            here = early.at[rows_of(j)]
            return remote(
                here, here, send_sem.at[j], early_recv.at[j], {"blk": target, "rep": rep}
            )

        def early_up_copy(j):
            return early_to(j, above * 2 + core, early_up)

        def early_down_copy(j):
            return early_to(j, below * 2 + core, early_down)

        def early_step(j, carry):
            @pl.when(is_owner)
            def _():
                early_load(j).wait()

            @pl.when(not_owner)
            def _():
                early_up_copy(j).wait_recv()

            @pl.when(jnp.logical_and(has_up, j < sent))
            def _():
                early_up_copy(j).start()

            @pl.when(jnp.logical_and(has_down, j < sent))
            def _():
                early_down_copy(j).start()

            return carry

        lax.fori_loop(0, jnp.where(is_owner, sent, held), early_step, 0)

        def early_finish(j, carry):
            @pl.when(has_up)
            def _():
                early_up_copy(j).wait_send()

            @pl.when(has_down)
            def _():
                early_down_copy(j).wait_send()

            return carry

    if reduces:
        load_own.wait()
        for copy in scatter:
            copy.wait()
        add_parts(part_own, part_recv, s_all, rep * part_rows)
        for copy in gather:
            copy.start()
        lax.fori_loop(middle, CHUNKS, step, 0)

    def finish(j, carry):
        @pl.when(jnp.logical_and(has_up, j >= first))
        def _():
            up(j).wait_send()

        @pl.when(jnp.logical_and(has_down, j >= first))
        def _():
            down(j).wait_send()

        pair(j).wait()
        return carry

    lax.fori_loop(0, CHUNKS, finish, 0)
    if reduces:
        for copy in gather:
            copy.wait()
    else:
        lax.fori_loop(0, sent, early_finish, 0)


def add_parts(part_own, part_recv, s_all, base):
    others, rows = part_recv.shape[:2]

    def step(i, carry):
        here = pl.ds(pl.multiple_of(i * ROW_BLOCK, ROW_BLOCK), ROW_BLOCK)
        total = part_own[here, :].astype(jnp.float32)
        for k in range(others):
            total = total + part_recv[k, here, :].astype(jnp.float32)
        there = pl.ds(pl.multiple_of(base + i * ROW_BLOCK, ROW_BLOCK), ROW_BLOCK)
        s_all[there, :] = total.astype(jnp.bfloat16)
        return carry

    lax.fori_loop(0, rows // ROW_BLOCK, step, 0)


def spread(features, partial, early, lane, chips, reps, per_rep):
    reduces = partial is not None
    node_rows, width = features.shape
    lanes = width // 2
    part_rows = node_rows // reps
    chunk_sem = pltpu.SemaphoreType.DMA((CHUNKS,))
    rep_sem = pltpu.SemaphoreType.DMA((reps - 1,))
    shape = jax.ShapeDtypeStruct
    anywhere = pl.BlockSpec(memory_space=pl.ANY)
    vmem = pl.BlockSpec(memory_space=pltpu.VMEM)
    args = [features]
    out_shape = [shape((per_rep, node_rows, lanes), features.dtype)]
    scratch = [chunk_sem] * 6
    if reduces:
        args += [partial, early]
        out_shape.append(shape((node_rows, lanes), features.dtype))
        scratch += [
            pltpu.VMEM((part_rows, lanes), jnp.bfloat16),
            pltpu.VMEM((reps - 1, part_rows, lanes), jnp.bfloat16),
            pltpu.SemaphoreType.DMA(()),
            rep_sem,
            rep_sem,
            rep_sem,
            rep_sem,
        ]
    else:
        out_shape.append(shape((node_rows, lanes), features.dtype))
        scratch += [chunk_sem] * 4
    return pl.pallas_call(
        functools.partial(spread_kernel, chips, reps, lane, reduces),
        out_shape=out_shape,
        in_specs=[anywhere] * len(args),
        out_specs=[vmem] * len(out_shape),
        scratch_shapes=scratch,
        compiler_params=pltpu.CompilerParams(
            collective_id=2 if reduces else 0, has_side_effects=True, vmem_limit_bytes=VMEM_LIMIT
        ),
    )(*args)


def tiles_kernel(count, rows, cols, tiles, sections, out, acc):
    slot = pl.program_id(0)
    side = tiles.shape[2]

    @pl.when(slot == 0)
    def _():
        acc[...] = jnp.zeros_like(acc)

    used = count[0, slot]

    def step(g, carry):
        terms = []
        for i in range(GROUP):
            m = g * GROUP + i
            col = pl.multiple_of(cols[0, slot, m] * side, side)
            term = product(tiles[0, m], sections[0, pl.ds(col, side), :])
            terms.append(jnp.where(m < used, term, 0.0))
        for i in range(GROUP):
            row = pl.multiple_of(rows[0, slot, g * GROUP + i] * side, side)
            acc[pl.ds(row, side), :] += terms[i]
        return carry

    lax.fori_loop(0, (used + GROUP - 1) // GROUP, step, 0)

    @pl.when(slot == pl.num_programs(0) - 1)
    def _():
        out[...] = acc[...].astype(out.dtype)


def tile_products(count, rows, cols, tiles, sections):
    per_rep, cap, side = tiles.shape[:3]
    node_rows, width = sections.shape[1:]
    return pl.pallas_call(
        tiles_kernel,
        out_shape=jax.ShapeDtypeStruct((node_rows, width), jnp.bfloat16),
        grid_spec=pltpu.PrefetchScalarGridSpec(
            num_scalar_prefetch=3,
            grid=(per_rep,),
            in_specs=[
                pl.BlockSpec((1, cap, side, side), lambda s, *_: (s, 0, 0, 0)),
                pl.BlockSpec((1, node_rows, width), lambda s, *_: (s, 0, 0)),
            ],
            out_specs=pl.BlockSpec((node_rows, width), lambda s, *_: (0, 0)),
            scratch_shapes=[pltpu.VMEM((node_rows, width), jnp.float32)],
        ),
        compiler_params=pltpu.CompilerParams(vmem_limit_bytes=VMEM_LIMIT),
    )(count, rows, cols, tiles, sections)


def cell_kernel(
    chips,
    reps,
    scale,
    partial,
    first_half,
    state_hbm,
    cot_hbm,
    w_graph,
    b_graph,
    w_input,
    w_state,
    w_cand,
    b_gates,
    new_state,
    state_grad,
    grads_out,
    state_v,
    cot_v,
    s_all,
    part_own,
    part_recv,
    grads,
    grads_b,
    half_recv,
    half_b,
    rep_recv,
    quarter_b,
    chip_recv,
    final,
    local_sem,
    rs_send,
    rs_recv,
    ag_send,
    ag_recv,
    pair_send,
    pair_recv,
    chip_send,
    chip_got,
    rep_send,
    rep_got,
    chip_send2,
    chip_got2,
    rep_send2,
    rep_got2,
):
    blk = lax.axis_index("blk")
    rep = lax.axis_index("rep")
    core = blk % 2
    chip = blk // 2
    width = w_cand.shape[0]
    part_rows = partial.shape[0] // reps
    half_rows = half_b.shape[0]
    quarter_rows = quarter_b.shape[0]
    piece_rows = chip_recv.shape[1]
    weight_rows = 7 * width

    def rep_at(k):
        return rep_shift(rep, reps, k)

    def on_rep(k):
        return {"blk": blk, "rep": rep_at(k)}

    def chip_at(k):
        return (chip + k) % chips

    def on_chip(k):
        return {"blk": chip_at(k) * 2 + core, "rep": rep}

    mate = {"blk": chip * 2 + 1 - core, "rep": rep}

    def part(index):
        return pl.ds(pl.multiple_of(index * part_rows, part_rows), part_rows)

    def piece(index):
        return pl.ds(pl.multiple_of(index * piece_rows, piece_rows), piece_rows)

    def quarter(index):
        return pl.ds(pl.multiple_of(index * quarter_rows, quarter_rows), quarter_rows)

    def half(index):
        return pl.ds(pl.multiple_of(index * half_rows, half_rows), half_rows)

    def remote(src, dst, send_sem, recv_sem, target):
        return pltpu.make_async_remote_copy(
            src_ref=src,
            dst_ref=dst,
            send_sem=send_sem,
            recv_sem=recv_sem,
            device_id=target,
            device_id_type=MESH,
        )

    loads = [
        pltpu.make_async_copy(partial.at[part(rep)], part_own, local_sem.at[0]),
        pltpu.make_async_copy(state_hbm, state_v, local_sem.at[1]),
        pltpu.make_async_copy(cot_hbm, cot_v, local_sem.at[2]),
    ]
    for load in loads:
        load.start()

    barrier = pltpu.get_barrier_semaphore()
    targets = [on_rep(k) for k in range(1, reps)] + [on_chip(k) for k in range(1, chips)] + [mate]
    for target in targets:
        pl.semaphore_signal(barrier, inc=1, device_id=target, device_id_type=MESH)
    pl.semaphore_wait(barrier, len(targets))

    own_base = rep * part_rows
    blocks = part_rows // ROW_BLOCK

    def block(base, i):
        return pl.ds(pl.multiple_of(base + i * ROW_BLOCK, ROW_BLOCK), ROW_BLOCK)

    def scatter(k, i):
        return remote(
            partial.at[block(rep_at(k) * part_rows, i)],
            part_recv.at[k - 1, block(0, i)],
            rs_send.at[k - 1, i],
            rs_recv.at[k - 1, i],
            on_rep(k),
        )

    def gather(k, i):
        rows = block(own_base, i)
        return remote(
            s_all.at[rows], s_all.at[rows], ag_send.at[k - 1, i], ag_recv.at[k - 1, i], on_rep(k)
        )

    def send_parts(i, carry):
        for k in reversed(range(1, reps)):
            scatter(k, i).start()
        return carry

    lax.fori_loop(0, blocks, send_parts, 0)
    grads[...] = jnp.zeros_like(grads)
    for load in loads:
        load.wait()

    def add_block(i):
        for k in range(1, reps):
            scatter(k, i).wait()
        here = block(0, i)
        total = part_own[here, :].astype(jnp.float32)
        for k in range(reps - 1):
            total = total + part_recv[k, here, :].astype(jnp.float32)
        s_all[block(own_base, i), :] = total.astype(jnp.bfloat16)
        for k in range(1, reps):
            gather(k, i).start()

    def cell(base, before, with_grads):
        def step(i, carry):
            before(i)
            here = block(base, i)
            summed_b = jnp.concatenate([first_half[here, :], s_all[here, :]], axis=1)
            state = state_v[here, :]
            graph_out = jnp.tanh(product(summed_b, w_graph[...]) + b_graph[...].reshape(1, -1))
            graph_b = graph_out.astype(jnp.bfloat16)
            from_input = product(graph_b, w_input[...]) + b_gates[...].reshape(1, -1)
            from_state = product(state, w_state[...])
            reset_gate = jax.nn.sigmoid(from_input[:, :width] + from_state[:, :width])
            update_gate = jax.nn.sigmoid(from_input[:, width : 2 * width] + from_state[:, width:])
            state_f = state.astype(jnp.float32)
            reset_state = (reset_gate * state_f).astype(jnp.bfloat16)
            candidate = jnp.tanh(from_input[:, 2 * width :] + product(reset_state, w_cand[...]))
            keep = 1.0 - update_gate
            new_state[here, :] = (update_gate * state_f + keep * candidate).astype(jnp.bfloat16)
            upstream = cot_v[here, :].astype(jnp.float32)
            grad_update = upstream * (state_f - candidate) * update_gate * keep
            grad_cand_f = upstream * keep * (1.0 - candidate * candidate)
            grad_cand_b = grad_cand_f.astype(jnp.bfloat16)
            grad_reset_state = contract_last(grad_cand_b, w_cand[...])
            grad_reset = grad_reset_state * state_f * reset_gate * (1.0 - reset_gate)
            gates_b = jnp.concatenate(
                [grad_reset.astype(jnp.bfloat16), grad_update.astype(jnp.bfloat16)], axis=1
            )
            state_grad[here, :] = (
                upstream * update_gate
                + grad_reset_state * reset_gate
                + contract_last(gates_b, w_state[...])
            ).astype(jnp.bfloat16)
            if with_grads:
                all_b = jnp.concatenate([gates_b, grad_cand_b], axis=1)
                grad_preact = contract_last(all_b, w_input[...]) * (1.0 - graph_out * graph_out)

                def add(at, value):
                    rows = pl.ds(at, value.shape[0])
                    grads[rows, :] += value

                add(0, contract_first(summed_b, grad_preact.astype(jnp.bfloat16)))
                to_input = contract_first(graph_b, all_b)
                for n in range(3):
                    add((1 + n) * width, to_input[:, n * width : (n + 1) * width])
                to_state = contract_first(state, gates_b)
                for n in range(2):
                    add((4 + n) * width, to_state[:, n * width : (n + 1) * width])
                add(6 * width, contract_first(reset_state, grad_cand_b))
                sums = [
                    jnp.sum(term, axis=0, keepdims=True)
                    for term in (grad_preact, grad_reset, grad_update, grad_cand_f)
                ]
                add(weight_rows, jnp.concatenate(sums + [jnp.zeros((4, width), jnp.float32)]))
            return carry

        lax.fori_loop(0, blocks, step, 0)

    cell(own_base, add_block, True)

    to_mate = remote(
        grads_b.at[half(1 - core)], half_recv, pair_send.at[0], pair_recv.at[0], mate
    )
    across = [
        remote(
            half_b.at[quarter(rep_at(k))],
            rep_recv.at[k - 1],
            rep_send.at[k - 1],
            rep_got.at[k - 1],
            on_rep(k),
        )
        for k in range(1, reps)
    ]
    between = [
        remote(
            quarter_b.at[piece(chip_at(k))],
            chip_recv.at[k - 1],
            chip_send.at[k - 1],
            chip_got.at[k - 1],
            on_chip(k),
        )
        for k in range(1, chips)
    ]
    quarter_base = core * half_rows + rep * quarter_rows
    mine = pl.ds(pl.multiple_of(quarter_base + chip * piece_rows, piece_rows), piece_rows)
    my_quarter = pl.ds(pl.multiple_of(quarter_base, quarter_rows), quarter_rows)
    back_chip = [
        remote(
            final.at[mine], final.at[mine], chip_send2.at[k - 1], chip_got2.at[k - 1], on_chip(k)
        )
        for k in range(1, chips)
    ]
    back_rep = [
        remote(
            final.at[my_quarter],
            final.at[my_quarter],
            rep_send2.at[k - 1],
            rep_got2.at[k - 1],
            on_rep(k),
        )
        for k in range(1, reps)
    ]

    def back_mate(k):
        base = core * half_rows + rep_origin(rep, reps, k) * quarter_rows
        rows = pl.ds(pl.multiple_of(base, quarter_rows), quarter_rows)
        return remote(
            final.at[rows], final.at[rows], pair_send.at[1 + k], pair_recv.at[1 + k], mate
        )

    def stage_pair():
        to_mate.wait()
        half_b[...] = (grads[half(core), :] + half_recv[...].astype(jnp.float32)).astype(
            jnp.bfloat16
        )
        for copy in across:
            copy.start()

    def stage_rep():
        for copy in across:
            copy.wait()
        total = half_b[quarter(rep), :].astype(jnp.float32)
        for k in range(reps - 1):
            total = total + rep_recv[k].astype(jnp.float32)
        quarter_b[...] = total.astype(jnp.bfloat16)
        for copy in between:
            copy.start()

    def stage_chip():
        for copy in between:
            copy.wait()
        total = quarter_b[piece(chip), :].astype(jnp.float32)
        for k in range(chips - 1):
            total = total + chip_recv[k].astype(jnp.float32)
        final[mine, :] = (total * scale).astype(jnp.bfloat16)
        for copy in back_chip:
            copy.start()

    def stage_back_chip():
        for copy in back_chip:
            copy.wait()
        for copy in back_rep:
            copy.start()
        back_mate(0).start()

    def stage_back_rep():
        for k in range(1, reps):
            back_rep[k - 1].wait()
            back_mate(k).start()

    grads_b[...] = grads[...].astype(jnp.bfloat16)
    to_mate.start()
    stage_pair()
    stages = [stage_rep, stage_chip, stage_back_chip, stage_back_rep]
    for k in range(1, reps):
        cell(rep_origin(rep, reps, k) * part_rows, lambda i: gather(k, i).wait(), False)
        if stages:
            stages.pop(0)()
    for stage in stages:
        stage()
    for k in range(reps):
        back_mate(k).wait()
    grads_out[...] = final[...]


def unpack_kernel(
    state_in,
    back_in,
    final,
    new_state,
    state_grad,
    grad_graph,
    graph_bias,
    grad_input,
    grad_state,
    grad_cand,
    gate_sums,
):
    new_state[...] = state_in[...]
    state_grad[...] = back_in[...]

    @pl.when(pl.program_id(0) == 0)
    def _():
        width = grad_cand.shape[0]

        def take(at, count):
            return final[pl.ds(at, count), :].astype(jnp.float32)

        grad_graph[...] = take(0, width)
        for n in range(3):
            grad_input[:, n * width : (n + 1) * width] = take((1 + n) * width, width)
        for n in range(2):
            grad_state[:, n * width : (n + 1) * width] = take((4 + n) * width, width)
        grad_cand[...] = take(6 * width, width)
        bias = take(7 * width, 16)
        graph_bias[...] = bias[0]
        for n in range(3):
            gate_sums[n * width : (n + 1) * width] = bias[1 + n]


def unpack(new_state, state_grad, final, width):
    node_rows = new_state.shape[0]
    rows = node_rows // 2
    f32, b16 = jnp.float32, jnp.bfloat16
    shape = jax.ShapeDtypeStruct
    block = pl.BlockSpec((rows, width), lambda i: (i, 0))
    whole = pl.BlockSpec(memory_space=pltpu.VMEM)
    return pl.pallas_call(
        unpack_kernel,
        grid=(node_rows // rows,),
        out_shape=[
            shape((node_rows, width), b16),
            shape((node_rows, width), b16),
            shape((width, width), f32),
            shape((width,), f32),
            shape((width, 3 * width), f32),
            shape((width, 2 * width), f32),
            shape((width, width), f32),
            shape((3 * width,), f32),
        ],
        in_specs=[block, block, whole],
        out_specs=[block, block] + [whole] * 6,
        compiler_params=pltpu.CompilerParams(vmem_limit_bytes=VMEM_LIMIT),
    )(new_state, state_grad, final)


def cell_step(partial, first_half, state, cotangent, weights, chips, reps):
    node_rows, width = state.shape
    lanes = partial.shape[1]
    blks = chips * 2
    unit = 16 * blks * reps
    grad_rows = (7 * width + 16 + unit - 1) // unit * unit
    half_rows = grad_rows // 2
    quarter_rows = half_rows // reps
    piece_rows = quarter_rows // chips
    part_rows = node_rows // reps
    scale = float(node_rows * blks) ** (-0.5)
    f32, b16 = jnp.float32, jnp.bfloat16
    shape = jax.ShapeDtypeStruct
    whole = pl.BlockSpec(memory_space=pltpu.VMEM)
    anywhere = pl.BlockSpec(memory_space=pl.ANY)
    dma = pltpu.SemaphoreType.DMA
    return pl.pallas_call(
        functools.partial(cell_kernel, chips, reps, scale),
        out_shape=[
            shape((node_rows, width), b16),
            shape((node_rows, width), b16),
            shape((grad_rows, width), b16),
        ],
        in_specs=[anywhere, whole, anywhere, anywhere] + [whole] * 6,
        out_specs=[whole] * 3,
        scratch_shapes=[
            pltpu.VMEM((node_rows, width), b16),
            pltpu.VMEM((node_rows, width), b16),
            pltpu.VMEM((node_rows, lanes), b16),
            pltpu.VMEM((part_rows, lanes), b16),
            pltpu.VMEM((reps - 1, part_rows, lanes), b16),
            pltpu.VMEM((grad_rows, width), f32),
            pltpu.VMEM((grad_rows, width), b16),
            pltpu.VMEM((half_rows, width), b16),
            pltpu.VMEM((half_rows, width), b16),
            pltpu.VMEM((reps - 1, quarter_rows, width), b16),
            pltpu.VMEM((quarter_rows, width), b16),
            pltpu.VMEM((chips - 1, piece_rows, width), b16),
            pltpu.VMEM((grad_rows, width), b16),
            dma((3,)),
            dma((reps - 1, part_rows // ROW_BLOCK)),
            dma((reps - 1, part_rows // ROW_BLOCK)),
            dma((reps - 1, part_rows // ROW_BLOCK)),
            dma((reps - 1, part_rows // ROW_BLOCK)),
            dma((1 + reps,)),
            dma((1 + reps,)),
            dma((chips - 1,)),
            dma((chips - 1,)),
            dma((reps - 1,)),
            dma((reps - 1,)),
            dma((chips - 1,)),
            dma((chips - 1,)),
            dma((reps - 1,)),
            dma((reps - 1,)),
        ],
        compiler_params=pltpu.CompilerParams(
            collective_id=1, has_side_effects=True, vmem_limit_bytes=VMEM_LIMIT
        ),
    )(partial, first_half, state, cotangent, *weights)


def solution(mesh):
    chips = mesh.shape["blk"] // 2
    reps = mesh.shape["rep"]

    def local(
        features,
        state,
        tiles,
        tile_count,
        tile_rows,
        tile_cols,
        w_graph,
        b_graph,
        w_input,
        w_state,
        w_cand,
        b_gates,
        cotangent,
    ):
        per_rep = tiles.shape[1]
        lanes = features.shape[1] // 2
        lists = (tile_count, tile_rows, tile_cols, tiles[0])
        sections, early = spread(features, None, None, 0, chips, reps, per_rep)
        partial = tile_products(*lists, sections)
        sections, first_half = spread(
            features, partial, early, lanes, chips, reps, per_rep
        )
        partial = tile_products(*lists, sections)
        weights = (w_graph, b_graph, w_input, w_state, w_cand, b_gates)
        outs = cell_step(partial, first_half, state, cotangent, weights, chips, reps)
        return tuple(unpack(*outs, w_cand.shape[0]))

    in_specs = (
        P("blk", None),
        P("blk", None),
        P("blk", "rep", None, None, None),
        P("blk", "rep"),
        P("blk", "rep", None),
        P("blk", "rep", None),
        P(),
        P(),
        P(),
        P(),
        P(),
        P(),
        P("blk", None),
    )
    out_specs = (P("blk", None), P("blk", None), P(), P(), P(), P(), P(), P())
    return jax.shard_map(local, mesh=mesh, in_specs=in_specs, out_specs=out_specs, check_vma=False)
```

profile of v0, /device:TPU:0, one launch (start us, length us, event | category | flops | bytes accessed | tf_op | source)
XLA Modules:
  0.0 139.9 jit_solution(14677153307191143923)
XLA Ops:
  0.6 39.0 %shard_map.188 = (bf16[2,4096,128]{2,1,0:T(8,128)(2,1)}, bf16[4096,128]{1,0:T(8,128)(2,1)}) custom-call(bf16[4096,256]{1,0:T(8,128)(2,1)} %refs_0_.3), custom_call_target="tpu_custom_call" | custom-call | tf_op jit(solution)/shard_map/pallas_call | solution.py:335
  39.7 6.5 %shard_map.189.refs_1_ = bf16[4096,128]{1,0:T(8,128)(2,1)} custom-call(s32[1,2]{1,0:T(1,128)} %count.3, s32[1,2,64]{2,1,0:T(2,128)} %rows.3, s32[1,2,64]{2,1,0:T(2,128)} %cols.3, bf16[2,64,128,128]{3,2,1,0:T(8,128)(2,1)} %bitcast.1, bf16[2,4096,128]{2,1,0:T(8,128)(2,1)} %get-tuple-element.15.sections), custom_call_target="tpu_custom_call" | custom-call | tf_op jit(solution)/shard_map/pallas_call | solution.py:379
  46.2 30.4 %shard_map.190 = (bf16[2,4096,128]{2,1,0:T(8,128)(2,1)}, bf16[4096,128]{1,0:T(8,128)(2,1)}) custom-call(bf16[4096,256]{1,0:T(8,128)(2,1)} %refs_0_.3, bf16[4096,128]{1,0:T(8,128)(2,1)} %shard_map.189.refs_1_, bf16[4096,128]{1,0:T(8,128)(2,1)} %get-tuple-element.16.refs_2_), custom_call_target="tpu_custom_call" | custom-call | tf_op jit(solution)/shard_map/pallas_call | solution.py:335
  76.6 6.5 %shard_map.191.partial = bf16[4096,128]{1,0:T(8,128)(2,1)} custom-call(s32[1,2]{1,0:T(1,128)} %count.3, s32[1,2,64]{2,1,0:T(2,128)} %rows.3, s32[1,2,64]{2,1,0:T(2,128)} %cols.3, bf16[2,64,128,128]{3,2,1,0:T(8,128)(2,1)} %bitcast.2, bf16[2,4096,128]{2,1,0:T(8,128)(2,1)} %get-tuple-element.17.sections), custom_call_target="tpu_custom_call" | custom-call | tf_op jit(solution)/shard_map/pallas_call | solution.py:379
  83.1 52.0 %shard_map.192 = (bf16[4096,256]{1,0:T(8,128)(2,1)}, bf16[4096,256]{1,0:T(8,128)(2,1)}, bf16[2048,256]{1,0:T(8,128)(2,1)}) custom-call(bf16[4096,128]{1,0:T(8,128)(2,1)} %shard_map.191.partial, bf16[4096,128]{1,0:T(8,128)(2,1)} %get-tuple-element.18.first_half, bf16[4096,256]{1,0:T(8,128)(2,1)} %state_hbm.1, bf16[4096,256]{1,0:T(8,128)(2,1)} %cot_hbm.1, ...), custom_call_target="tpu_custom_call" | custom-call | tf_op jit(solution)/shard_map/pallas_call | solution.py:785
  135.1 4.7 %shard_map.193 = (bf16[4096,256]{1,0:T(8,128)(2,1)}, bf16[4096,256]{1,0:T(8,128)(2,1)}, f32[256,256]{1,0:T(8,128)}, f32[256]{0:T(256)}, f32[256,768]{1,0:T(8,128...) custom-call(bf16[4096,256]{1,0:T(8,128)(2,1)} %get-tuple-element.19.state_in, ...), custom_call_target="tpu_custom_call" | custom-call | tf_op jit(solution)/shard_map/pallas_call | solution.py:750
where the time goes:
time: 140 us
  Pallas kernels  139 us (99%)
    pallas_call x2, Pallas kernels, spread(): pl.pallas_call(functools.partial(spread_kernel, chips, reps, lane, reduce...  69.4 us
    pallas_call x1, Pallas kernels, cell_step(): pl.pallas_call(functools.partial(cell_kernel, chips, reps, scale), out_sh...  52 us
    pallas_call x2, Pallas kernels, tile_products(): pl.pallas_call(tiles_kernel, out_shape=jax.ShapeDtypeStruct((node_rows, w...  13 us
    pallas_call x1, Pallas kernels, unpack(): pl.pallas_call(unpack_kernel, grid=(node_rows // rows,), out_shape=[shape...  4.72 us

commit v1 on v0

--- a/solution.py
+++ b/solution.py
@@ -346,29 +346,31 @@
 
 def tiles_kernel(count, rows, cols, tiles, sections, out, acc):
     slot = pl.program_id(0)
-    side = tiles.shape[2]
-
-    @pl.when(slot == 0)
+    span = pl.program_id(1)
+    held, side = tiles.shape[1:3]
+    base = span * held
+
+    @pl.when(jnp.logical_and(slot == 0, span == 0))
     def _():
         acc[...] = jnp.zeros_like(acc)
 
-    used = count[0, slot]
+    used = jnp.clip(count[0, slot] - base, 0, held)
 
     def step(g, carry):
         terms = []
         for i in range(GROUP):
             m = g * GROUP + i
-            col = pl.multiple_of(cols[0, slot, m] * side, side)
+            col = pl.multiple_of(cols[0, slot, base + m] * side, side)
             term = product(tiles[0, m], sections[0, pl.ds(col, side), :])
             terms.append(jnp.where(m < used, term, 0.0))
         for i in range(GROUP):
-            row = pl.multiple_of(rows[0, slot, g * GROUP + i] * side, side)
+            row = pl.multiple_of(rows[0, slot, base + g * GROUP + i] * side, side)
             acc[pl.ds(row, side), :] += terms[i]
         return carry
 
     lax.fori_loop(0, (used + GROUP - 1) // GROUP, step, 0)
 
-    @pl.when(slot == pl.num_programs(0) - 1)
+    @pl.when(jnp.logical_and(slot == pl.num_programs(0) - 1, span == pl.num_programs(1) - 1))
     def _():
         out[...] = acc[...].astype(out.dtype)
 
@@ -381,12 +383,12 @@
         out_shape=jax.ShapeDtypeStruct((node_rows, width), jnp.bfloat16),
         grid_spec=pltpu.PrefetchScalarGridSpec(
             num_scalar_prefetch=3,
-            grid=(per_rep,),
+            grid=(per_rep, 2),
             in_specs=[
-                pl.BlockSpec((1, cap, side, side), lambda s, *_: (s, 0, 0, 0)),
-                pl.BlockSpec((1, node_rows, width), lambda s, *_: (s, 0, 0)),
+                pl.BlockSpec((1, cap // 2, side, side), lambda s, h, *_: (s, h, 0, 0)),
+                pl.BlockSpec((1, node_rows, width), lambda s, h, *_: (s, 0, 0)),
             ],
-            out_specs=pl.BlockSpec((node_rows, width), lambda s, *_: (0, 0)),
+            out_specs=pl.BlockSpec((node_rows, width), lambda s, h, *_: (0, 0)),
             scratch_shapes=[pltpu.VMEM((node_rows, width), jnp.float32)],
         ),
         compiler_params=pltpu.CompilerParams(vmem_limit_bytes=VMEM_LIMIT),

time: 140 us -> 144 us (1.029)
  Pallas kernels: 139 us -> 143 us
    pallas_call x2, Pallas kernels: 13 us -> 15.5 us  [tile_products(): pl.pallas_call(tiles_kernel, out_shape=jax.ShapeDtypeStruct((node_rows, w...]
    pallas_call x2, Pallas kernels: 69.4 us -> 71.1 us  [spread(): pl.pallas_call(functools.partial(spread_kernel, chips, reps, lane, reduce...]
where the time goes in v1:
time: 144 us; the launch traced here: 143 us
  Pallas kernels  143 us (99%)
    pallas_call x2, Pallas kernels, spread(): pl.pallas_call(functools.partial(spread_kernel, chips, reps, lane, reduce...  71.1 us
    pallas_call x1, Pallas kernels, cell_step(): pl.pallas_call(functools.partial(cell_kernel, chips, reps, scale), out_sh...  51.5 us
    pallas_call x2, Pallas kernels, tile_products(): pl.pallas_call(tiles_kernel, out_shape=jax.ShapeDtypeStruct((node_rows, w...  15.5 us
    pallas_call x1, Pallas kernels, unpack(): pl.pallas_call(unpack_kernel, grid=(node_rows // rows,), out_shape=[shape...  4.72 us

profile of v1, /device:TPU:0, one launch (start us, length us, event | category | flops | bytes accessed | tf_op | source)
XLA Modules:
  0.0 143.5 jit_solution(4633920455481794487)
XLA Ops:
  0.6 39.0 %shard_map.188 = (bf16[2,4096,128]{2,1,0:T(8,128)(2,1)}, bf16[4096,128]{1,0:T(8,128)(2,1)}) custom-call(bf16[4096,256]{1,0:T(8,128)(2,1)} %refs_0_.3), custom_call_target="tpu_custom_call" | custom-call | tf_op jit(solution)/shard_map/pallas_call | solution.py:335
  39.7 7.7 %shard_map.189.refs_1_ = bf16[4096,128]{1,0:T(8,128)(2,1)} custom-call(s32[1,2]{1,0:T(1,128)} %count.3, s32[1,2,64]{2,1,0:T(2,128)} %rows.3, s32[1,2,64]{2,1,0:T(2,128)} %cols.3, bf16[2,64,128,128]{3,2,1,0:T(8,128)(2,1)} %bitcast.1, bf16[2,4096,128]{2,1,0:T(8,128)(2,1)} %get-tuple-element.15.sections), custom_call_target="tpu_custom_call" | custom-call | tf_op jit(solution)/shard_map/pallas_call | solution.py:381
  47.4 32.0 %shard_map.190 = (bf16[2,4096,128]{2,1,0:T(8,128)(2,1)}, bf16[4096,128]{1,0:T(8,128)(2,1)}) custom-call(bf16[4096,256]{1,0:T(8,128)(2,1)} %refs_0_.3, bf16[4096,128]{1,0:T(8,128)(2,1)} %shard_map.189.refs_1_, bf16[4096,128]{1,0:T(8,128)(2,1)} %get-tuple-element.16.refs_2_), custom_call_target="tpu_custom_call" | custom-call | tf_op jit(solution)/shard_map/pallas_call | solution.py:335
  79.5 7.8 %shard_map.191.partial = bf16[4096,128]{1,0:T(8,128)(2,1)} custom-call(s32[1,2]{1,0:T(1,128)} %count.3, s32[1,2,64]{2,1,0:T(2,128)} %rows.3, s32[1,2,64]{2,1,0:T(2,128)} %cols.3, bf16[2,64,128,128]{3,2,1,0:T(8,128)(2,1)} %bitcast.2, bf16[2,4096,128]{2,1,0:T(8,128)(2,1)} %get-tuple-element.17.sections), custom_call_target="tpu_custom_call" | custom-call | tf_op jit(solution)/shard_map/pallas_call | solution.py:381
  87.2 51.5 %shard_map.192 = (bf16[4096,256]{1,0:T(8,128)(2,1)}, bf16[4096,256]{1,0:T(8,128)(2,1)}, bf16[2048,256]{1,0:T(8,128)(2,1)}) custom-call(bf16[4096,128]{1,0:T(8,128)(2,1)} %shard_map.191.partial, bf16[4096,128]{1,0:T(8,128)(2,1)} %get-tuple-element.18.first_half, bf16[4096,256]{1,0:T(8,128)(2,1)} %state_hbm.1, bf16[4096,256]{1,0:T(8,128)(2,1)} %cot_hbm.1, ...), custom_call_target="tpu_custom_call" | custom-call | tf_op jit(solution)/shard_map/pallas_call | solution.py:787
  138.8 4.7 %shard_map.193 = (bf16[4096,256]{1,0:T(8,128)(2,1)}, bf16[4096,256]{1,0:T(8,128)(2,1)}, f32[256,256]{1,0:T(8,128)}, f32[256]{0:T(256)}, f32[256,768]{1,0:T(8,128...) custom-call(bf16[4096,256]{1,0:T(8,128)(2,1)} %get-tuple-element.19.state_in, ...), custom_call_target="tpu_custom_call" | custom-call | tf_op jit(solution)/shard_map/pallas_call | solution.py:752
